TPU v7x, 32 devices: a whole 2x2x4 slice. The times are simulated.
32 devices in a mesh: dp: 4 (over z), tensor: 8 (over y, x, core).
Axes of the slice: x: 2, y: 2, z: 4, core: 2. Of those that a mesh axis runs over, the one named last changes fastest.
Arguments:
- hidden: bfloat16 [3584, 4096], P('dp', 'tensor')
- gain: bfloat16 [4096], P('tensor'), may hold values from 0.5 to 1.5
- head_weight: bfloat16 [4096, 32000], P('dp', 'tensor')
- targets: int32 [3584], P('dp'), may hold values from 0 to 31999
- seq_ids: int32 [3584], P(('dp', 'tensor')), may hold values from 0 to 15, never falling along the last dimension, each value on 1 to 1792 neighbouring positions
- live: int32 [3584], P(('dp', 'tensor')), may hold values 0 or 1
Outputs:
- logprob: float32 [3584], P(('dp', 'tensor'))
- entropy: float32 [3584], P(('dp', 'tensor'))
- seq_mean: float32 [16], replicated
Inputs may be any that keep to these rules, and one draw needn't show every extreme that they name: `seq_ids`: sequence numbers never fall along the tokens; each sequence has 1 to 1792 tokens, one exactly 1792.
All inputs are finite; a program needn't handle non-finite values. No bound on the sum of `live` on one device may be relied on, other than what follows from the above.
Results may differ from a plain program's by a relative error of at most 0.0015.
Values may be sent and summed in bfloat16 or wider, within the bound.
A program may use at most 128 MiB of HBM per device.

v0:
```python
import jax
import jax.numpy as jnp
from jax import lax
from jax.sharding import PartitionSpec as P

SEQ_DEV = 4


def body(hidden, gain, head_weight, targets, seq_ids, live):
    shards = lax.axis_size("tensor")
    rank = lax.axis_index("tensor")
    tok_rows = hidden.shape[0]
    share = tok_rows // shards
    vocab_dev = head_weight.shape[1]
    whole, gains = (
        lax.all_gather(hidden, "tensor", axis=1, tiled=True),
        lax.all_gather(gain, "tensor", axis=0, tiled=True),
    )
    values = whole.astype(jnp.float32)
    meansq = jnp.mean(values * values, axis=-1, keepdims=True)
    normed = (values * lax.rsqrt(meansq + 1e-05) * gains.astype(jnp.float32)).astype(jnp.bfloat16)
    scores = jnp.dot(
        normed,
        lax.all_gather(head_weight, "dp", axis=0, tiled=True),
        preferred_element_type=jnp.float32,
    )
    top = jnp.max(scores, axis=-1)
    shifted = scores - top[:, None]
    expo = jnp.exp(shifted)
    total = jnp.sum(expo, axis=-1)
    spread = jnp.sum(expo * shifted, axis=-1)
    local_ids = targets - rank * vocab_dev
    inside = (local_ids >= 0) & (local_ids < vocab_dev)
    picked = jnp.take_along_axis(scores, jnp.clip(local_ids, 0, vocab_dev - 1)[:, None], axis=1)[
        :, 0
    ]
    target_score = jnp.where(inside, picked, 0.0)
    offset = rank * share
    best = lax.pmax(top, "tensor")
    scale = jnp.exp(top - best)
    sums = lax.psum(
        (total * scale, (spread + (top - best) * total) * scale, target_score), "tensor"
    )
    g_top = lax.dynamic_slice_in_dim(best, offset, share, 0)
    g_total = lax.dynamic_slice_in_dim(sums[0], offset, share, 0)
    g_spread = lax.dynamic_slice_in_dim(sums[1], offset, share, 0)
    g_target = lax.dynamic_slice_in_dim(sums[2], offset, share, 0)
    weight = live.astype(jnp.float32)
    log_total = jnp.log(g_total)
    logprob = (g_target - g_top - log_total) * weight
    entropy = (log_total - g_spread / g_total) * weight
    seq_count = SEQ_DEV * lax.axis_size("dp")
    member = (seq_ids[:, None] == jnp.arange(seq_count)[None, :]).astype(jnp.float32)
    seq_sums = jnp.sum(member * logprob[:, None], axis=0)
    seq_live = jnp.sum(member * weight[:, None], axis=0)
    seq_sums, seq_live = lax.psum((seq_sums, seq_live), ("dp", "tensor"))
    seq_mean = seq_sums / jnp.maximum(seq_live, 1.0)
    return (logprob, entropy, seq_mean)


def solution(mesh):
    placed = (
        P("dp", "tensor"),
        P("tensor"),
        P("dp", "tensor"),
        P("dp"),
        P(("dp", "tensor")),
        P(("dp", "tensor")),
    )
    return jax.shard_map(
        body,
        mesh=mesh,
        in_specs=placed,
        out_specs=(P(("dp", "tensor")), P(("dp", "tensor")), P()),
        check_vma=False,
    )
```

profile of v0, /device:TPU:10, one launch (start us, length us, event | category | flops | bytes accessed | tf_op | source)
XLA Modules:
  0.0 776.8 jit_solution(17668721989190920865)
XLA Ops:
  7.2 0.0 all-gather.4.cloned.1.call-start
  7.2 0.7 all-gather.4.cloned.1.call-update
  7.9 0.0 all-gather.6.cloned.1.call-start
  7.9 0.7 all-gather.6.cloned.1.call-update
  8.7 0.7 reshape.51
  9.3 8.9 %all-gather = bf16[8,1,512]{2,1,0:T(2,128)(2,1)S(1)} all-gather(bf16[1,1,512]{2,1,0:T(2,128)(2,1)S(1)} %reshape.51), channel_id=1, replica_groups=mesh['dp'=4,'tensor'=8] {'tensor'}, dimensions={0}, use_global_device_ids=true | all-gather | bytes 9216 | tf_op jit(solution)/shard_map/all_gather | solution.py:17
  18.3 0.7 compare_select_fusion
  19.0 0.7 convert_element_type.16
  19.7 42.7 %all-gather.4.cloned.1.call-done = bf16[896,4096]{1,0:T(8,128)(2,1)} async-done(((bf16[896,512]{1,0:T(8,128)(2,1)}), bf16[896,4096]{1,0:T(8,128)(2,1)}) %all-gather.4.cloned.1.call-update) | async-done | bytes 7340048 | tf_op jit(solution)/shard_map/all_gather | solution.py:16
  62.4 4.6 fusion
  66.9 542.8 %all-gather.6.cloned.1.call-done = bf16[4096,4000]{0,1:T(8,128)(2,1)} async-done(((bf16[1024,4000]{0,1:T(8,128)(2,1)}), bf16[4096,4000]{0,1:T(8,128)(2,1)}) %all-gather.6.cloned.1.call-update) | async-done | bytes 32768016 | tf_op jit(solution)/shard_map/all_gather | solution.py:24
  609.8 41.9 %fusion.12 = (f32[896]{0:T(1024)S(1)}, f32[896,4000]{0,1:T(8,128)}) fusion(bf16[4096,4000]{0,1:T(8,128)(2,1)} %all-gather.6.cloned.1.call-done, bf16[896,4096]{1,0:T(8,128)(2,1)} %all-gather.4.cloned.1.call-done, f32[4096]{0:T(1024)S(1)} %bitcast.4, f32[896]{0:T(1024)S(1)} %add_rsqrt_fusion), kind=kOutput, calls=%fused_computation.30 | convolution fusion | flops 29378392064 | bytes 54467584 | tf_op jit(solution)/shard_map/dot_general | solution.py:22
  651.7 11.2 %pmax.7 = f32[896]{0:T(1024)S(1)} all-reduce(f32[896]{0:T(1024)S(1)} %get-tuple-element.16), channel_id=1, replica_groups=mesh['dp'=4,'tensor'=8] {'tensor'}, use_global_device_ids=true, to_apply=%region_3.0 | all-reduce | flops 896 | bytes 7168 | tf_op jit(solution)/shard_map/pmax | solution.py:39
  662.9 7.9 %fusion.3 = (f32[896]{0:T(1024)S(1)}, f32[896]{0:T(1024)S(1)}) fusion(f32[896,4000]{0,1:T(8,128)} %get-tuple-element.17, f32[896]{0:T(1024)S(1)} %get-tuple-element.16), kind=kLoop, calls=%fused_computation.8 | loop fusion | flops 14334208 | bytes 14346752 | tf_op jit(solution)/shard_map/reduce_sum | solution.py:31
  670.8 25.8 %gather_fusion = f32[896]{0:T(1024)S(1)} fusion(f32[896,4000]{0,1:T(8,128)} %get-tuple-element.17, s32[896]{0:T(1024)S(1)} %fusion.11), kind=kCustom, calls=%fused_computation | custom fusion | bytes 14336 | tf_op jit(solution)/shard_map/jit(take_along_axis)/gather | solution.py:34
  696.6 0.0 copy-done
  696.7 27.1 %all-reduce.1 = (f32[896]{0:T(1024)S(1)}, f32[896]{0:T(1024)S(1)}, f32[896]{0:T(1024)S(1)}) all-reduce(f32[896]{0:T(1024)S(1)} %select_select_fusion, f32[896]{0:T(1024)S(1)} %get-tuple-element.13, f32[896]{0:T(1024)S(1)} %get-tuple-element.12), channel_id=1, replica_groups=mesh['dp'=4,'tensor'=8] {'tensor'}, use_global_device_ids=true, to_apply=%region_1.0 | all-reduce | flops 2688 | bytes 21504 | tf_op jit(solution)/shard_map/psum | solution.py:41
  723.7 0.0 copy-done.3
  723.7 0.6 subtract_multiply_fusion
  724.3 0.0 copy-done.2
  724.3 0.1 select_reduce_fusion
  724.4 45.0 %all-reduce = (f32[16]{0:T(128)S(1)}, f32[16]{0:T(128)S(1)}) all-reduce(f32[16]{0:T(128)S(1)} %get-tuple-element.6, f32[16]{0:T(128)S(1)} %get-tuple-element.5), channel_id=1, replica_groups=mesh['dp'=4,'tensor'=8] {'dp','tensor'}, use_global_device_ids=true, to_apply=%region_9.10 | all-reduce | flops 32 | bytes 256 | tf_op jit(solution)/shard_map/psum | solution.py:56
  769.5 0.5 maximum_divide_fusion
  770.0 0.0 copy-done.1
  (12 shorter events, 0.1 us)
Async XLA Ops:
  7.2 55.2 %all-gather.4.cloned.1.call-start = ((), (), s32[]{:S(2)}) async-start(), calls=%async_computation | async-start | bytes 8257536 | tf_op jit(solution)/shard_map/all_gather | solution.py:16
  7.9 601.9 %all-gather.6.cloned.1.call-start = ((), (), s32[]{:S(2)}) async-start(), calls=%async_computation.1 | async-start | bytes 40960000 | tf_op jit(solution)/shard_map/all_gather | solution.py:24
  651.7 44.9 %copy-start = (s32[896]{0:T(1024)S(1)}, s32[896]{0:T(1024)}, u32[]{:S(2)}) copy-start(s32[896]{0:T(1024)} %param.9) | copy-start | bytes 10756
  651.7 72.1 %copy-start.3 = (s32[112]{0:T(128)S(1)}, s32[112]{0:T(128)}, u32[]{:S(2)}) copy-start(s32[112]{0:T(128)} %param.11) | copy-start | bytes 1348
  651.7 72.7 %copy-start.2 = (s32[112]{0:T(128)S(1)}, s32[112]{0:T(128)}, u32[]{:S(2)}) copy-start(s32[112]{0:T(128)} %param.10) | copy-start | bytes 1348
  724.3 45.6 %copy-start.1 = (f32[112]{0:T(128)}, f32[112]{0:T(128)S(1)}, u32[]{:S(2)}) copy-start(f32[112]{0:T(128)S(1)} %get-tuple-element.15) | copy-start | bytes 1348
Sparse Core Ops, SparseCore 0:
  9.9 52.4 all-gather.3
  63.9 545.7 all-gather.5
where the time goes:
time: 777 us
  waiting for transfers between devices  587 us (76%)
  blocking collectives  92.2 us (12%)
  matrix products  41.9 us (5%)
  local copies, waits for them, and re-layouts  26.5 us (3%)
  other arithmetic  15.2 us (2%)
  between operations  14.1 us (2%)
    all_gather x1, waiting for transfers between devices, body(): lax.all_gather(head_weight, 'dp', axis=0, tiled=True)  543 us
    psum x1, blocking collectives, body(): seq_sums, seq_live = lax.psum((seq_sums, seq_live), ('dp', 'tensor'))  45 us
    all_gather x1, waiting for transfers between devices, body(): lax.all_gather(hidden, 'tensor', axis=1, tiled=True)  42.7 us
    dot_general x1, matrix products, body(): jnp.dot(normed, lax.all_gather(head_weight, 'dp', axis=0, tiled=True), pr...  41.9 us
    psum x1, blocking collectives, body(): lax.psum((total * scale, (spread + (top - best) * total) * scale, target_...  27.1 us
    gather x1, local copies, waits for them, and re-layouts, body(): jnp.take_along_axis(scores, jnp.clip(local_ids, 0, vocab_dev - 1)[:, None...  25.8 us
  transfers between devices with their start and end apart: 2, of which 2 were waited for; matrix products, arithmetic and copies ran while one was open for 1% of the time, Pallas kernels for 0%

commit v1 on v0

v1 whole, which is shorter than its diff:
```python
import functools

import jax
import jax.numpy as jnp
from jax import lax
from jax.experimental import pallas as pl
from jax.experimental.pallas import tpu as pltpu
from jax.sharding import PartitionSpec as P

SEQ_DEV = 4
GROUP = 4
MESH = pl.DeviceIdType.MESH


def window(vocab_dev, group):
    part = vocab_dev // group
    for align in (16, 8):
        starts = [part * p // align * align for p in range(group)]
        need = max(part * (p + 1) - s for p, s in enumerate(starts))
        length = -(-need // align) * align
        if all(s + length <= vocab_dev for s in starts):
            return part, align, length
    raise ValueError("shard")


def pieces(length, align, many):
    units = length // align
    sizes = [(units // many + (i < units % many)) * align for i in range(many)]
    out, at = [], 0
    for s in sizes:
        out.append((at, s))
        at += s
    return out


def kernel(
    cfg,
    hid, gain, wt, targets, seq_ids, live,
    logprob, entropy, seq_mean,
    x, w, tgt, sq_out, sq_in, st, st_out, st_in, sq_seq_out, sq_seq_in,
    w_send, w_recv, w_loc, z_send, z_recv, p_send, p_recv, s_send, s_recv, g_send, g_recv, m_send, m_recv,
):
    (dp, tn, g, part, align, length, chunks, tile) = cfg
    z, t = lax.axis_index("dp"), lax.axis_index("tensor")
    p = lax.rem(z, g)
    zb = z - p
    R, Dl = hid.shape
    Kl = wt.shape[1]
    chips = tn // 2
    N = dp * tn
    me = z * tn + t
    share = R // tn
    seqs = seq_mean.shape[0]

    def remote(src, dst, ss, rs, zz, tt):
        return pltpu.make_async_remote_copy(
            src_ref=src, dst_ref=dst, send_sem=ss, recv_sem=rs,
            device_id={"dp": zz, "tensor": tt}, device_id_type=MESH,
        )

    barrier = pltpu.get_barrier_semaphore()

    @pl.loop(1, N)
    def _(d):
        o = lax.rem(me + d, N)
        pl.semaphore_signal(
            barrier, inc=1, device_id={"dp": o // tn, "tensor": lax.rem(o, tn)}, device_id_type=MESH
        )

    pl.semaphore_wait(barrier, N - 1)

    def start_of(pp):
        return pl.multiple_of(part * pp // align * align, align)

    def w_copy(d, c, to, frm):
        off, size = chunks[c]
        return remote(
            wt.at[pl.ds(start_of(lax.rem(to, g)) + off, size)],
            w.at[pl.ds(off, size), pl.ds(pl.multiple_of(frm * Kl, Kl), Kl)],
            w_send.at[d - 1, c], w_recv.at[d - 1, c], to, t,
        )

    def w_own(c):
        off, size = chunks[c]
        return pltpu.make_async_copy(
            wt.at[pl.ds(start_of(p) + off, size)],
            w.at[pl.ds(off, size), pl.ds(pl.multiple_of(z * Kl, Kl), Kl)],
            w_loc.at[c],
        )

    def start_w(c):
        for d in range(1, dp):
            w_copy(d, c, lax.rem(z + d, dp), z).start()
        w_own(c).start()

    values = hid[...].astype(jnp.float32)
    sums = jnp.sum(values * values, axis=-1, keepdims=True)
    sq_out[...] = jnp.transpose(jnp.broadcast_to(sums, (R, 128)))[:8, :]

    def sq_copy(d, slot):
        return remote(sq_out, sq_in.at[slot], m_send.at[0], m_recv.at[0], z, lax.rem(t + d, tn))

    @pl.loop(1, tn)
    def _(d):
        sq_copy(d, t).start()

    sq_in[t] = sq_out[...]

    def tgt_copy(d, slot):
        return remote(
            targets, tgt.at[slot], g_send.at[d - 1], g_recv.at[d - 1], zb + lax.rem(p + d, g), t
        )

    for d in range(1, g):
        tgt_copy(d, p).start()
    tgt[p] = targets[...]
    for c in range(len(chunks)):
        start_w(c)

    pltpu.make_async_copy(
        sq_in.at[pl.ds(0, tn - 1)], sq_in.at[pl.ds(0, tn - 1)], m_recv.at[0]
    ).wait()
    square = jnp.sum(sq_in[...], axis=0)
    wide = jnp.transpose(jnp.concatenate([square] * 16, axis=0))
    scale = lax.rsqrt(wide / (tn * Dl) + 1e-05)
    rows0 = pl.ds(pl.multiple_of(p * R, R), R)
    for i in range(Dl // 128):
        cut = slice(i * 128, (i + 1) * 128)
        x[rows0, pl.ds(pl.multiple_of(t * Dl + i * 128, 128), 128)] = (
            values[:, cut] * scale * gain[:, cut].astype(jnp.float32)
        ).astype(jnp.bfloat16)

    def block(k, tt):
        return x.at[pl.ds(pl.multiple_of(k * R, R), R), pl.ds(pl.multiple_of(tt * Dl, Dl), Dl)]

    def z_copy(k, way):
        step = 1 if way == 0 else -1
        return remote(block(k, t), block(k, t), z_send.at[way, k], z_recv.at[k], z + step, t)

    def p_copy(k, j, src):
        return remote(
            block(k, src), block(k, src), p_send.at[k, j - 1], p_recv.at[k, j - 1], z, t ^ (2 * j)
        )

    def s_copy(k, j, src):
        return remote(block(k, src), block(k, src), s_send.at[k, j], s_recv.at[k, j], z, t ^ 1)

    def spread_out(k):
        for j in range(1, chips):
            p_copy(k, j, t).start()
        s_copy(k, 0, t).start()

    def gather_in(k):
        for j in range(1, chips):
            p_copy(k, j, t ^ (2 * j)).wait_recv()
            s_copy(k, j, t ^ (2 * j)).start()

    def each(s, fn):
        if s == 0:
            fn(p, None)
            return

        @pl.when(p - s >= 0)
        def _():
            fn(p - s, 0)

        @pl.when(p + s < g)
        def _():
            fn(p + s, 1)

    def arrive(k, way):
        if way is not None:
            z_copy(k, way).wait_recv()
        if way in (None, 0):

            @pl.when(p < g - 1)
            def _():
                z_copy(k, 0).start()

        if way in (None, 1):

            @pl.when(p > 0)
            def _():
                z_copy(k, 1).start()

        spread_out(k)

    each(0, arrive)
    for s in range(1, g):
        each(s, arrive)
        each(s - 1, lambda k, way: gather_in(k))
    each(g - 1, lambda k, way: gather_in(k))

    @pl.loop(0, g)
    def _(k):
        for j in range(chips):
            s_copy(k, j, t ^ 1 ^ (2 * j)).wait_recv()

    for d in range(1, g):
        tgt_copy(d, lax.rem(p - d + g, g)).wait_recv()

    first = t * (g * part) + start_of(p)
    low = p * part - start_of(p)
    for c, (off, size) in enumerate(chunks):
        w_own(c).wait()
        for d in range(1, dp):
            w_copy(d, c, z, lax.rem(z - d + dp, dp)).wait_recv()

        @pl.loop(0, R // tile * g)
        def _(b):
            k = b // (R // tile)
            lane = pl.multiple_of(lax.rem(b, R // tile) * tile, tile)
            scores = lax.dot_general(
                w[pl.ds(off, size), :],
                x[pl.ds(pl.multiple_of(b * tile, tile), tile), :],
                (((1,), (1,)), ((), ())),
                preferred_element_type=jnp.float32,
            )
            row = lax.broadcasted_iota(jnp.int32, (size, 1), 0) + off
            edge = c in (0, len(chunks) - 1)
            if edge:
                inside = (row >= low) & (row < low + part)
                top = jnp.max(jnp.where(inside, scores, -jnp.inf), axis=0, keepdims=True)
            else:
                top = jnp.max(scores, axis=0, keepdims=True)
            local = tgt[k, :, pl.ds(lane, tile)] - first
            local = jnp.where((local >= low) & (local < low + part), local, -1)
            picked = jnp.sum(jnp.where(row == local, scores, 0.0), axis=0, keepdims=True)
            if c > 0:
                was = st[k, 0:1, pl.ds(lane, tile)]
                top = jnp.maximum(top, was)
            shifted = scores - top
            if edge:
                shifted = jnp.where(inside, shifted, -1e4)
            expo = jnp.exp(shifted)
            total = jnp.sum(expo, axis=0, keepdims=True)
            spread = jnp.sum(expo * shifted, axis=0, keepdims=True)
            if c > 0:
                fall = was - top
                by = jnp.exp(fall)
                t0 = st[k, 1:2, pl.ds(lane, tile)]
                total += t0 * by
                spread += (st[k, 2:3, pl.ds(lane, tile)] + fall * t0) * by
                picked += st[k, 3:4, pl.ds(lane, tile)]
            st[k, 0:1, pl.ds(lane, tile)] = top
            st[k, 1:2, pl.ds(lane, tile)] = total
            st[k, 2:3, pl.ds(lane, tile)] = spread
            st[k, 3:4, pl.ds(lane, tile)] = picked

    n = g * tn
    mine = p * tn + t
    for k in range(g):
        for i in range(tn):
            st_out[k * tn + i, :, 0:share] = st[k, :, i * share : (i + 1) * share]

    def st_copy(o, slot):
        return remote(
            st_out.at[o], st_in.at[slot], m_send.at[1], m_recv.at[1], zb + o // tn, lax.rem(o, tn)
        )

    @pl.loop(1, n)
    def _(d):
        st_copy(lax.rem(mine + d, n), mine).start()

    st_in[mine] = st_out[mine]
    pltpu.make_async_copy(
        st_in.at[pl.ds(0, n - 1)], st_in.at[pl.ds(0, n - 1)], m_recv.at[1]
    ).wait()
    got = st_in[...]
    tops = got[:, 0:1, 0:share]
    best = jnp.max(tops, axis=0)
    fall = tops - best[None]
    by = jnp.exp(fall)
    total = jnp.sum(got[:, 1:2, 0:share] * by, axis=0)
    spread = jnp.sum((got[:, 2:3, 0:share] + fall * got[:, 1:2, 0:share]) * by, axis=0)
    picked = jnp.sum(got[:, 3:4, 0:share], axis=0)
    weight = live[...].astype(jnp.float32)
    log_total = jnp.log(total)
    logp = (picked - best - log_total) * weight
    logprob[...] = logp
    entropy[...] = (log_total - spread / total) * weight

    member = lax.broadcasted_iota(jnp.int32, (seqs, share), 0) == seq_ids[...]
    s_sum = jnp.sum(jnp.where(member, logp, 0.0), axis=1, keepdims=True)
    s_live = jnp.sum(jnp.where(member, weight, 0.0), axis=1, keepdims=True)
    lanes = lax.broadcasted_iota(jnp.int32, (seqs, 128), 1)
    both = jnp.where(lanes < 64, s_sum, s_live)
    sq_seq_out[...] = both

    def seq_copy(d, slot):
        o = lax.rem(me + d, N)
        return remote(
            sq_seq_out, sq_seq_in.at[slot], m_send.at[2], m_recv.at[2], o // tn, lax.rem(o, tn)
        )

    @pl.loop(1, N)
    def _(d):
        seq_copy(d, me).start()

    sq_seq_in[me] = both
    pltpu.make_async_copy(
        sq_seq_in.at[pl.ds(0, N - 1)], sq_seq_in.at[pl.ds(0, N - 1)], m_recv.at[2]
    ).wait()
    sums_all = jnp.sum(sq_seq_in[...], axis=0)
    seq_mean[...] = sums_all[:, 0:1] / jnp.maximum(sums_all[:, 64:65], 1.0)

    pltpu.make_async_copy(sq_in.at[pl.ds(0, tn - 1)], sq_in.at[pl.ds(0, tn - 1)], m_send.at[0]).wait()
    pltpu.make_async_copy(st_in.at[pl.ds(0, n - 1)], st_in.at[pl.ds(0, n - 1)], m_send.at[1]).wait()
    pltpu.make_async_copy(
        sq_seq_in.at[pl.ds(0, N - 1)], sq_seq_in.at[pl.ds(0, N - 1)], m_send.at[2]
    ).wait()
    for d in range(1, g):
        tgt_copy(d, p).wait_send()
    for c in range(len(chunks)):
        for d in range(1, dp):
            w_copy(d, c, lax.rem(z + d, dp), z).wait_send()

    def sent(k, way):
        if way in (None, 0):

            @pl.when(p < g - 1)
            def _():
                z_copy(k, 0).wait_send()

        if way in (None, 1):

            @pl.when(p > 0)
            def _():
                z_copy(k, 1).wait_send()

    for s in range(g):
        each(s, sent)

    @pl.loop(0, g)
    def _(k):
        for j in range(chips):
            if j:
                p_copy(k, j, t).wait_send()
            s_copy(k, j, t ^ (2 * j)).wait_send()


def body(dp, tn, hidden, gain, head_weight, targets, seq_ids, live):
    g = GROUP if dp % GROUP == 0 else 1
    R, Dl = hidden.shape
    D = Dl * tn
    Kl, vocab_dev = head_weight.shape
    part, align, length = window(vocab_dev, g)
    chunks = pieces(length, align, max(1, length // 240))
    share = R // tn
    seqs = SEQ_DEV * dp
    N = dp * tn
    chips = tn // 2
    tile = max((n for n in range(128, 1025, 128) if R % n == 0), default=R)
    cfg = (dp, tn, g, part, align, length, chunks, tile)
    f32, dma = jnp.float32, pltpu.SemaphoreType.DMA
    vm = pl.BlockSpec(memory_space=pltpu.VMEM)
    nc = len(chunks)
    logprob, entropy, seq_mean = pl.pallas_call(
        functools.partial(kernel, cfg),
        out_shape=(
            jax.ShapeDtypeStruct((1, share), f32),
            jax.ShapeDtypeStruct((1, share), f32),
            jax.ShapeDtypeStruct((seqs, 1), f32),
        ),
        in_specs=[vm, vm, pl.BlockSpec(memory_space=pl.ANY), vm, vm, vm],
        out_specs=(vm, vm, vm),
        scratch_shapes=[
            pltpu.VMEM((g * R, D), jnp.bfloat16),
            pltpu.VMEM((length, D), jnp.bfloat16),
            pltpu.VMEM((g, 1, R), jnp.int32),
            pltpu.VMEM((8, R), f32),
            pltpu.VMEM((tn, 8, R), f32),
            pltpu.VMEM((g, 8, R), f32),
            pltpu.VMEM((g * tn, 8, 128), f32),
            pltpu.VMEM((g * tn, 8, 128), f32),
            pltpu.VMEM((seqs, 128), f32),
            pltpu.VMEM((N, seqs, 128), f32),
            dma((dp - 1, nc)), dma((dp - 1, nc)), dma((nc,)),
            dma((2, g)), dma((g,)),
            dma((g, chips)), dma((g, chips)),
            dma((g, chips)), dma((g, chips)),
            dma((max(g - 1, 1),)), dma((max(g - 1, 1),)),
            dma((3,)), dma((3,)),
        ],
        compiler_params=pltpu.CompilerParams(
            collective_id=0, has_side_effects=True, vmem_limit_bytes=60 * 2**20
        ),
        cost_estimate=pl.CostEstimate(
            flops=2 * g * R * length * D, bytes_accessed=2 * length * D, transcendentals=g * R * length
        ),
    )(
        hidden,
        gain.reshape(1, Dl),
        head_weight.T,
        targets.reshape(1, R),
        seq_ids.reshape(1, share),
        live.reshape(1, share),
    )
    return logprob.reshape(share), entropy.reshape(share), seq_mean.reshape(seqs)


def solution(mesh):
    placed = (
        P("dp", "tensor"),
        P("tensor"),
        P("dp", "tensor"),
        P("dp"),
        P(("dp", "tensor")),
        P(("dp", "tensor")),
    )
    return jax.shard_map(
        functools.partial(body, mesh.shape["dp"], mesh.shape["tensor"]),
        mesh=mesh,
        in_specs=placed,
        out_specs=(P(("dp", "tensor")), P(("dp", "tensor")), P()),
        check_vma=False,
    )
```

time: 777 us -> 390 us (0.50)
  waiting for transfers between devices: 587 us -> 0 us
  Pallas kernels: 0 us -> 382 us
  blocking collectives: 92.2 us -> 0 us
  matrix products: 41.9 us -> 0 us
  local copies, waits for them, and re-layouts: 26.5 us -> 4.84 us
  other arithmetic: 15.2 us -> 1.32 us
  between operations: 14.1 us -> 0.64 us
    all_gather x2 -> x0, waiting for transfers between devices: 586 us -> none  [the longest x1 543 us: body(): lax.all_gather(head_weight, 'dp', axis=0, tiled=True)]
    pallas_call x0 -> x1, Pallas kernels: none -> 382 us  [body(): pl.pallas_call(functools.partial(kernel, cfg), out_shape=(jax.ShapeDtypeS...]
    psum x2 -> x0, blocking collectives: 72.1 us -> none  [the longest x1 45 us: body(): seq_sums, seq_live = lax.psum((seq_sums, seq_live), ('dp', 'tensor'))]
    dot_general x1 -> x0, matrix products: 41.9 us -> none  [body(): jnp.dot(normed, lax.all_gather(head_weight, 'dp', axis=0, tiled=True), pr...]
    gather x1 -> x0, local copies, waits for them, and re-layouts: 25.8 us -> none  [body(): jnp.take_along_axis(scores, jnp.clip(local_ids, 0, vocab_dev - 1)[:, None...]
    reduce_sum x3 -> x0, other arithmetic: 12.6 us -> none  [the longest x1 7.93 us: body(): spread = jnp.sum(expo * shifted, axis=-1)]
    pmax x1 -> x0, blocking collectives: 11.2 us -> none  [body(): best = lax.pmax(top, 'tensor')]
    all_gather x1 -> x0, blocking collectives: 8.89 us -> none  [body(): lax.all_gather(gain, 'tensor', axis=0, tiled=True)]
  transfers between devices with their start and end apart: 2 -> 0, of which waited for: 2 -> 0; matrix products, arithmetic and copies ran while one was open for 1% -> 0% of each run, Pallas kernels for 0% -> 0%
where the time goes in v1:
time: 390 us; the launch traced here: 389 us
  Pallas kernels  382 us (98%)
  local copies, waits for them, and re-layouts  4.84 us (1%)
    pallas_call x1, Pallas kernels, body(): pl.pallas_call(functools.partial(kernel, cfg), out_shape=(jax.ShapeDtypeS...  382 us

profile of v1, /device:TPU:10, one launch (start us, length us, event | category | flops | bytes accessed | tf_op | source)
XLA Modules:
  0.0 389.0 jit_solution(1107072348106272761)
XLA Ops:
  0.6 1.2 reshape.27.gain
  1.9 1.3 reshape.28.targets
  3.1 382.2 %shard_map.85 = (f32[1,112]{1,0:T(1,128)}, f32[1,112]{1,0:T(1,128)}, f32[16,1]{1,0:T(8,128)}) custom-call(bf16[896,512]{1,0:T(8,128)(2,1)} %hid.1, bf16[1,512]{1,0:T(2,128)(2,1)} %reshape.27.gain, bf16[4000,1024]{1,0:T(8,128)(2,1)} %bitcast.5, s32[1,896]{1,0:T(1,128)} %reshape.28.targets, s32[1,112]{1,0:T(1,128)} %bitcast.6, s32[1,112]{1,0:T(1,128)} %bitcast.7), custom_call_target="tpu_custom_call" | custom-call | flops 29595009024 | bytes 8257536 | tf_op jit(solution)/shard_map/pallas_call | solution.py:358
  385.4 1.3 reduce
  386.7 1.2 copy.11
  387.9 1.1 copy.12

commit v2 on v1

--- a/solution.py
+++ b/solution.py
@@ -23,14 +23,15 @@
     raise ValueError("shard")
 
 
-def pieces(length, align, many):
-    units = length // align
-    sizes = [(units // many + (i < units % many)) * align for i in range(many)]
-    out, at = [], 0
-    for s in sizes:
-        out.append((at, s))
-        at += s
-    return out
+SHARES = (5, 7, 7, 7, 13, 13, 11)
+WORK = ((0, 1, 2, 3), (4,), (5,), (6,))
+
+
+def pieces(length, align):
+    units, edges = length // align, [0]
+    for i in range(len(SHARES)):
+        edges.append(units * sum(SHARES[: i + 1]) // sum(SHARES))
+    return [(a * align, (b - a) * align) for a, b in zip(edges, edges[1:])]
 
 
 def kernel(
@@ -114,14 +115,12 @@
     for d in range(1, g):
         tgt_copy(d, p).start()
     tgt[p] = targets[...]
-    for c in range(len(chunks)):
-        start_w(c)
-
+    start_w(0)
     pltpu.make_async_copy(
         sq_in.at[pl.ds(0, tn - 1)], sq_in.at[pl.ds(0, tn - 1)], m_recv.at[0]
     ).wait()
-    square = jnp.sum(sq_in[...], axis=0)
-    wide = jnp.transpose(jnp.concatenate([square] * 16, axis=0))
+    squares = jnp.sum(sq_in[...], axis=0)
+    wide = jnp.transpose(jnp.concatenate([squares] * 16, axis=0))
     scale = lax.rsqrt(wide / (tn * Dl) + 1e-05)
     rows0 = pl.ds(pl.multiple_of(p * R, R), R)
     for i in range(Dl // 128):
@@ -145,15 +144,30 @@
     def s_copy(k, j, src):
         return remote(block(k, src), block(k, src), s_send.at[k, j], s_recv.at[k, j], z, t ^ 1)
 
+    square = chips == 4 and R % 32 == 0
+    direct = (1, 2) if square else tuple(range(1, chips))
+
+    def half_copy(k, h, src):
+        at = block(k, src).at[pl.ds(h * (R // 2), R // 2)]
+        return remote(at, at, p_send.at[k, 2 + h], p_recv.at[k, 2 + h], z, t ^ (4 if h == 0 else 2))
+
     def spread_out(k):
-        for j in range(1, chips):
+        for j in direct:
             p_copy(k, j, t).start()
         s_copy(k, 0, t).start()
 
     def gather_in(k):
-        for j in range(1, chips):
+        for j in direct:
             p_copy(k, j, t ^ (2 * j)).wait_recv()
+            if square:
+                half_copy(k, j - 1, t ^ (2 * j)).start()
             s_copy(k, j, t ^ (2 * j)).start()
+
+    def gather_last(k):
+        if square:
+            for h in (0, 1):
+                half_copy(k, h, t ^ 6).wait_recv()
+            s_copy(k, 3, t ^ 6).start()
 
     def each(s, fn):
         if s == 0:
@@ -186,10 +200,17 @@
         spread_out(k)
 
     each(0, arrive)
+    late = 1
     for s in range(1, g):
+        start_w(late)
+        late += 1
         each(s, arrive)
         each(s - 1, lambda k, way: gather_in(k))
+    for c in range(late, len(chunks)):
+        start_w(c)
     each(g - 1, lambda k, way: gather_in(k))
+    for s in range(g):
+        each(s, lambda k, way: gather_last(k))
 
     @pl.loop(0, g)
     def _(k):
@@ -201,10 +222,12 @@
 
     first = t * (g * part) + start_of(p)
     low = p * part - start_of(p)
-    for c, (off, size) in enumerate(chunks):
-        w_own(c).wait()
-        for d in range(1, dp):
-            w_copy(d, c, z, lax.rem(z - d + dp, dp)).wait_recv()
+    for c, members in enumerate(WORK):
+        for i in members:
+            w_own(i).wait()
+            for d in range(1, dp):
+                w_copy(d, i, z, lax.rem(z - d + dp, dp)).wait_recv()
+        off, size = chunks[members[0]][0], sum(chunks[i][1] for i in members)
 
         @pl.loop(0, R // tile * g)
         def _(b):
@@ -217,7 +240,7 @@
                 preferred_element_type=jnp.float32,
             )
             row = lax.broadcasted_iota(jnp.int32, (size, 1), 0) + off
-            edge = c in (0, len(chunks) - 1)
+            edge = c in (0, len(WORK) - 1)
             if edge:
                 inside = (row >= low) & (row < low + part)
                 top = jnp.max(jnp.where(inside, scores, -jnp.inf), axis=0, keepdims=True)
@@ -334,9 +357,11 @@
     @pl.loop(0, g)
     def _(k):
         for j in range(chips):
-            if j:
-                p_copy(k, j, t).wait_send()
             s_copy(k, j, t ^ (2 * j)).wait_send()
+        for j in direct:
+            p_copy(k, j, t).wait_send()
+            if square:
+                half_copy(k, j - 1, t ^ (2 * j)).wait_send()
 
 
 def body(dp, tn, hidden, gain, head_weight, targets, seq_ids, live):
@@ -345,7 +370,7 @@
     D = Dl * tn
     Kl, vocab_dev = head_weight.shape
     part, align, length = window(vocab_dev, g)
-    chunks = pieces(length, align, max(1, length // 240))
+    chunks = pieces(length, align)
     share = R // tn
     seqs = SEQ_DEV * dp
     N = dp * tn
@@ -377,7 +402,7 @@
             pltpu.VMEM((N, seqs, 128), f32),
             dma((dp - 1, nc)), dma((dp - 1, nc)), dma((nc,)),
             dma((2, g)), dma((g,)),
-            dma((g, chips)), dma((g, chips)),
+            dma((g, max(chips, 4))), dma((g, max(chips, 4))),
             dma((g, chips)), dma((g, chips)),
             dma((max(g - 1, 1),)), dma((max(g - 1, 1),)),
             dma((3,)), dma((3,)),

time: 390 us -> 263 us (0.67)
  Pallas kernels: 382 us -> 255 us
    pallas_call x1, Pallas kernels: 382 us -> 255 us  [body(): pl.pallas_call(functools.partial(kernel, cfg), out_shape=(jax.ShapeDtypeS...]
where the time goes in v2:
time: 263 us; the launch traced here: 262 us
  Pallas kernels  255 us (97%)
  local copies, waits for them, and re-layouts  4.84 us (2%)
    pallas_call x1, Pallas kernels, body(): pl.pallas_call(functools.partial(kernel, cfg), out_shape=(jax.ShapeDtypeS...  255 us

profile of v2, /device:TPU:10, one launch (start us, length us, event | category | flops | bytes accessed | tf_op | source)
XLA Modules:
  0.0 262.0 jit_solution(10886026647263011346)
XLA Ops:
  0.6 1.2 reshape.27.gain
  1.9 1.3 reshape.28.targets
  3.1 255.2 %shard_map.85 = (f32[1,112]{1,0:T(1,128)}, f32[1,112]{1,0:T(1,128)}, f32[16,1]{1,0:T(8,128)}) custom-call(bf16[896,512]{1,0:T(8,128)(2,1)} %hid.1, bf16[1,512]{1,0:T(2,128)(2,1)} %reshape.27.gain, bf16[4000,1024]{1,0:T(8,128)(2,1)} %bitcast.5, s32[1,896]{1,0:T(1,128)} %reshape.28.targets, s32[1,112]{1,0:T(1,128)} %bitcast.6, s32[1,112]{1,0:T(1,128)} %bitcast.7), custom_call_target="tpu_custom_call" | custom-call | flops 29595009024 | bytes 8257536 | tf_op jit(solution)/shard_map/pallas_call | solution.py:383
  258.4 1.3 reduce
  259.7 1.2 copy.11
  260.9 1.1 copy.12
